TPU v7x, 32 devices: a whole 2x2x4 slice. The times are simulated.
32 devices in a mesh: sy: 4 (over z), sx: 4 (over y, core), tp: 2 (over x).
Axes of the slice: x: 2, y: 2, z: 4, core: 2. Of those that a mesh axis runs over, the one named last changes fastest.
Arguments:
- features: bfloat16 [96, 64, 1408], P('sy', 'sx', 'tp'), may hold values from -6 to 6
- depth_kernel: float32 [7, 7, 1408], P(None, None, 'tp'), may hold values from -0.875 to 0.875
- depth_bias: float32 [1408], P('tp'), may hold values from -1 to 1
- norm_gain: float32 [1408], replicated, may hold values from 0.1 to 1.9
- norm_bias: float32 [1408], replicated, may hold values from -3 to 3
- up_weight: bfloat16 [1408, 5632], P(None, 'tp'), may hold values from -0.15625 to 0.15625
- up_bias: float32 [5632], P('tp'), may hold values from -3 to 3
- response_gain: float32 [5632], P('tp'), may hold values from -4 to 4
- response_shift: float32 [5632], P('tp'), may hold values from -3 to 3
- down_weight: bfloat16 [5632, 1408], P('tp', ('sy', 'sx')), may hold values from -0.078125 to 0.078125
- down_bias: float32 [1408], P('tp'), may hold values from -3 to 3
- tissue: int32 [12, 8], P('sy', 'sx'), may hold values from 0 to 1, as said below
- cotangent: bfloat16 [96, 64, 1408], P('sy', 'sx', 'tp'), may hold values from -6 to 6
Outputs:
- block_out: bfloat16 [96, 64, 1408], P('sy', 'sx', 'tp')
- feature_grad: bfloat16 [96, 64, 1408], P('sy', 'sx', 'tp')
Inputs may be any that keep to these rules, and one draw needn't show every extreme that they name: Each device's block of 3 x 2 tiles holds 1 to 4 tissue tiles; some device's block holds exactly 4.
All inputs are finite; a program needn't handle non-finite values.
Results may differ from a plain program's by a relative error of at most 0.0049.
The roundings to bfloat16 on the way count: a program that leaves them out, or rounds other values in their place, can miss the bound.
Values may be sent and summed in bfloat16 or wider, within the bound.
A program may use at most 128 MiB of HBM per device.

v0:
```python
import jax
import jax.numpy as jnp
from jax import lax
from jax.sharding import PartitionSpec as P

KERNEL = 7
TILE = 8
root_half = 0.7071067811865476
root_two_pi_inv = 0.3989422804014327


def extended(block, sides, width):
    for axis, dim in sides:
        count = lax.axis_size(axis)
        forward = [(i, i + 1) for i in range(count - 1)]
        backward = [(target, source) for source, target in forward]
        low = lax.ppermute(
            lax.slice_in_dim(block, block.shape[dim] - width, None, axis=dim), axis, forward
        )
        high = lax.ppermute(lax.slice_in_dim(block, 0, width, axis=dim), axis, backward)
        block = jnp.concatenate([low, block, high], axis=dim)
    return block


def gelu_value(values):
    return 0.5 * values * (1.0 + jax.scipy.special.erf(values * root_half))


def gelu_slope(values):
    return (
        0.5 * (1.0 + jax.scipy.special.erf(values * root_half))
        + values * jnp.exp(-0.5 * values * values) * root_two_pi_inv
    )


def depthwise(padded, kernel, rows_out, cols_out, flipped):
    summed = jnp.zeros((rows_out, cols_out, kernel.shape[2]), jnp.float32)
    last_tap = KERNEL - 1
    for row_tap in range(KERNEL):
        for col_tap in range(KERNEL):
            row_start = last_tap - row_tap if flipped else row_tap
            col_start = last_tap - col_tap if flipped else col_tap
            window = padded[row_start : row_start + rows_out, col_start : col_start + cols_out]
            summed = summed + window.astype(jnp.float32) * kernel[row_tap, col_tap]
    return summed


MOST = 4


def extend(image):
    return extended(image, (("sy", 0), ("sx", 1)), KERNEL // 2)


def swapped(array):
    count = lax.axis_size("tp")
    return lax.ppermute(array, "tp", [(i, count - 1 - i) for i in range(count)])


def over_pixels(vector):
    return lax.psum(vector, ("sy", "sx"))


def conv_tiles(windows, kernel):
    summed = jnp.zeros((windows.shape[0], TILE, TILE, windows.shape[3]), jnp.float32)
    for row_tap in range(KERNEL):
        for col_tap in range(KERNEL):
            window = windows[:, row_tap : row_tap + TILE, col_tap : col_tap + TILE]
            summed = summed + window.astype(jnp.float32) * kernel[row_tap, col_tap]
    return summed


def shards(
    features,
    depth_kernel,
    depth_bias,
    norm_gain,
    norm_bias,
    up_weight,
    up_bias,
    response_gain,
    response_shift,
    down_weight,
    down_bias,
    tissue,
    cotangent,
):
    image_rows, image_cols, local_channels = features.shape
    tiles_y, tiles_x = tissue.shape
    tiles = tiles_y * tiles_x
    channels = up_weight.shape[0]
    hidden_total = up_weight.shape[1] * lax.axis_size("tp")
    tp_index = lax.axis_index("tp")
    first = tp_index == 0
    channel_start = tp_index * local_channels
    other_start = (1 - tp_index) * local_channels
    contract_last = (((1,), (1,)), ((), ()))
    pixels = MOST * TILE * TILE
    down_t = lax.all_gather(down_weight.T, ("sy", "sx"), axis=0, tiled=True)
    flags = tissue.reshape(-1)
    tile_ids = jnp.arange(tiles, dtype=jnp.int32)
    earlier = (tile_ids[None, :] < tile_ids[:, None]).astype(jnp.int32)
    ahead = jnp.sum(earlier * flags[None, :], axis=1)
    slot_of = jnp.where(flags > 0, ahead, jnp.sum(flags) + tile_ids - ahead)
    chosen = [jnp.sum(jnp.where(slot_of == s, tile_ids, 0)) for s in range(MOST)]
    slot_mask = jnp.stack([jnp.sum(jnp.where(slot_of == s, flags, 0)) for s in range(MOST)])
    mask_rows = jnp.repeat(slot_mask, TILE * TILE).astype(jnp.float32)

    def windows_of(image, side):
        return jnp.stack(
            [
                lax.dynamic_slice(
                    image,
                    (t // tiles_x * TILE, t % tiles_x * TILE, 0),
                    (side, side, image.shape[2]),
                )
                for t in chosen
            ]
        )

    def spread_out(rows_array):
        held = rows_array.reshape(MOST, TILE, TILE, rows_array.shape[1])
        held = jnp.concatenate([held, jnp.zeros_like(held[:1])], axis=0)
        slots = jnp.minimum(slot_of, MOST)
        rows = []
        for ty in range(tiles_y):
            row = [
                lax.dynamic_index_in_dim(held, slots[ty * tiles_x + tx], 0, keepdims=False)
                for tx in range(tiles_x)
            ]
            rows.append(jnp.concatenate(row, axis=1))
        return jnp.concatenate(rows, axis=0)

    def both_halves(own):
        other = swapped(own)
        return jnp.where(
            first, jnp.concatenate([own, other], axis=1), jnp.concatenate([other, own], axis=1)
        )

    cot_tiles = windows_of(cotangent, TILE).reshape(pixels, local_channels)
    masked_cot = (cot_tiles.astype(jnp.float32) * mask_rows[:, None]).astype(jnp.bfloat16)
    cot_wide = both_halves(masked_cot)
    convolved = conv_tiles(windows_of(extend(features), TILE + KERNEL - 1), depth_kernel)
    convolved = (convolved + depth_bias).astype(jnp.bfloat16).reshape(pixels, local_channels)
    gathered = both_halves(convolved).astype(jnp.float32)
    centre = jnp.mean(gathered, axis=1, keepdims=True)
    spread = jnp.mean(jnp.square(gathered - centre), axis=1, keepdims=True)
    inv_scale = lax.rsqrt(spread + 1e-06)
    standard = (gathered - centre) * inv_scale
    normed = (standard * norm_gain + norm_bias).astype(jnp.bfloat16)
    preact = jnp.dot(normed, up_weight, preferred_element_type=jnp.float32) + up_bias
    hidden = gelu_value(preact).astype(jnp.bfloat16)
    hidden_wide = hidden.astype(jnp.float32)
    squares = over_pixels(jnp.sum(mask_rows[:, None] * hidden_wide * hidden_wide, axis=0))
    column_norms = jnp.sqrt(squares)
    norms_here = jnp.full((8, 128), jnp.sum(column_norms))
    norm_level = (norms_here + swapped(norms_here))[0, 0] / hidden_total + 1e-06
    norm_ratio = column_norms / norm_level
    back_hidden = jnp.dot(cot_wide, down_t, preferred_element_type=jnp.float32)
    products = over_pixels(jnp.sum(back_hidden * hidden_wide, axis=0))
    response = (response_gain * hidden_wide * norm_ratio + response_shift + hidden_wide).astype(
        jnp.bfloat16
    )
    partial_out = lax.dot_general(
        response, down_t, contract_last, preferred_element_type=jnp.float32
    )
    sent_out = lax.dynamic_slice_in_dim(partial_out, other_start, local_channels, 1)
    kept_out = lax.dynamic_slice_in_dim(partial_out, channel_start, local_channels, 1)
    branch = kept_out + swapped(sent_out.astype(jnp.bfloat16)).astype(jnp.float32)
    ratio_grad = response_gain * products
    dots_here = jnp.full((8, 128), jnp.sum(ratio_grad * column_norms))
    dots = (dots_here + swapped(dots_here))[0, 0]
    norms_grad = ratio_grad / norm_level - dots / (hidden_total * norm_level * norm_level)
    hidden_grad = (
        back_hidden * (response_gain * norm_ratio + 1.0)
        + norms_grad * mask_rows[:, None] * hidden_wide / column_norms
    )
    preact_grad = (hidden_grad * gelu_slope(preact)).astype(jnp.bfloat16)
    grad_terms = lax.dot_general(
        preact_grad, up_weight, contract_last, preferred_element_type=jnp.float32
    )
    scaled_terms = grad_terms * norm_gain
    sums_here = jnp.stack([jnp.sum(scaled_terms, axis=1), jnp.sum(scaled_terms * standard, axis=1)])
    sums = sums_here + swapped(sums_here)
    sent_grad = lax.dynamic_slice_in_dim(scaled_terms, other_start, local_channels, 1)
    kept_grad = lax.dynamic_slice_in_dim(scaled_terms, channel_start, local_channels, 1)
    own_standard = lax.dynamic_slice_in_dim(standard, channel_start, local_channels, 1)
    scaled = kept_grad + swapped(sent_grad.astype(jnp.bfloat16)).astype(jnp.float32)
    convolved_grad = inv_scale * (
        scaled - (sums[0] / channels)[:, None] - own_standard * (sums[1] / channels)[:, None]
    )
    grad_image = spread_out(convolved_grad.astype(jnp.bfloat16))
    feature_grad = (
        cotangent.astype(jnp.float32)
        + depthwise(extend(grad_image), depth_kernel, image_rows, image_cols, True)
    ).astype(jnp.bfloat16)
    addend = spread_out(mask_rows[:, None] * (branch + down_bias))
    block_out = (features.astype(jnp.float32) + addend).astype(jnp.bfloat16)
    return (block_out, feature_grad)


def solution(mesh):
    placed = (
        P("sy", "sx", "tp"),
        P(None, None, "tp"),
        P("tp"),
        P(),
        P(),
        P(None, "tp"),
        P("tp"),
        P("tp"),
        P("tp"),
        P("tp", ("sy", "sx")),
        P("tp"),
        P("sy", "sx"),
        P("sy", "sx", "tp"),
    )
    return jax.shard_map(
        shards,
        mesh=mesh,
        in_specs=placed,
        out_specs=(P("sy", "sx", "tp"), P("sy", "sx", "tp")),
        check_vma=False,
    )
```

profile of v0, /device:TPU:12, one launch (start us, length us, event | category | flops | bytes accessed | tf_op | source)
XLA Modules:
  0.0 235.3 jit_solution(2763965542860036640)
XLA Ops:
  7.9 1.0 fusion.105
  8.9 3.6 %collective-permute-start = (bf16[3,16,704]{2,1,0:T(8,128)(2,1)S(1)}, bf16[3,16,704]{2,1,0:T(8,128)(2,1)S(1)}, u32[]{:S(2)}, u32[]{:S(2)}) collective-permute-start(bf16[3,16,704]{2,1,0:T(8,128)(2,1)S(1)} %get-tuple-element.90), channel_id=1, source_target_pairs={{0,8},{8,16},{16,24},{1,9},{9,17},{17,25},{2,10},{10,18},{18,26},{... | collective-permute-start | bytes 202760 | tf_op jit(solution)/shard_map/ppermute | solution.py:17
  12.5 2.4 %collective-permute-start.1 = (bf16[3,16,704]{2,1,0:T(8,128)(2,1)S(1)}, bf16[3,16,704]{2,1,0:T(8,128)(2,1)S(1)}, u32[]{:S(2)}, u32[]{:S(2)}) collective-permute-start(bf16[3,16,704]{2,1,0:T(8,128)(2,1)S(1)} %get-tuple-element.89), channel_id=1, source_target_pairs={{8,0},{16,8},{24,16},{9,1},{17,9},{25,17},{10,2},{18,10},{26,18},{... | collective-permute-start | bytes 202760 | tf_op jit(solution)/shard_map/ppermute | solution.py:20
  15.9 1.3 reduce_sum.166
  28.8 2.7 %add_convert_fusion.4 = f32[4]{0:T(128)S(1)} fusion(s32[1]{0:T(128)} %bitcast.3, s32[1]{0:T(128)} %bitcast.2, s32[1]{0:T(128)} %bitcast.1, s32[1]{0:T(128)} %bitcast), kind=kLoop, calls=%fused_computation.313 | loop fusion | flops 16 | bytes 32 | tf_op jit(solution)/shard_map/convert_element_type | solution.py:107
  32.4 1.9 collective-permute-start.2
  34.3 3.6 %collective-permute-start.3 = (bf16[30,3,704]{2,1,0:T(4,128)(2,1)S(1)}, bf16[30,3,704]{2,1,0:T(4,128)(2,1)S(1)}, u32[]{:S(2)}, u32[]{:S(2)}) collective-permute-start(bf16[30,3,704]{2,1,0:T(4,128)(2,1)S(1)} %get-tuple-element.86), channel_id=1, source_target_pairs={{2,0},{4,2},{6,4},{3,1},{5,3},{7,5},{10,8},{12,10},{14,12},{11,9},... | collective-permute-start | bytes 380168 | tf_op jit(solution)/shard_map/ppermute | solution.py:20
  38.1 1.1 collective-permute-done.2
  39.2 1.8 collective-permute-done.3
  43.0 5.8 %add_convert_fusion.2 = bf16[4,8,8,704]{3,2,1,0:T(8,128)(2,1)S(1)} fusion(bf16[4,14,14,704]{3,2,1,0:T(8,128)(2,1)S(1)} %pad_maximum_fusion, f32[704]{0:T(1024)S(1)} %copy-done.4, f32[704]{0:T(1024)S(1)} %get-tuple-element.53, f32[704]{0:T(1024)S(1)} %get-tuple-element.54, f32[704]{0:T(1024)S(1)} %get-tuple-element.7, f32[704]{0:T(1024)S(1)} %get-tuple-element.8, ...), kind=kLoop, calls=%fused_computation.138 | loop fusion | flops 26673152 | bytes 18163200 | tf_op jit(solution)/shard_map/convert_element_type | solution.py:144
  48.8 1.6 collective-permute-start.4
  51.8 9.1 %collective-permute-done.4 = bf16[256,704]{1,0:T(8,128)(2,1)S(1)} collective-permute-done((bf16[256,704]{1,0:T(8,128)(2,1)S(1)}, bf16[256,704]{1,0:T(8,128)(2,1)S(1)}, u32[]{:S(2)}, u32[]{:S(2)}) %collective-permute-start.4) | collective-permute-done | bytes 360480 | tf_op jit(solution)/shard_map/ppermute | solution.py:57
  62.2 7.7 %convolution_add_fusion = f32[256,2816]{1,0:T(8,128)} fusion(bf16[1408,2816]{1,0:T(8,128)(2,1)} %param.18, f32[2816]{0:T(1024)S(1)} %copy-done.6, f32[1408]{0:T(1024)S(1)} %copy-done.8, f32[1408]{0:T(1024)S(1)} %copy-done.9, f32[256]{0:T(256)S(1)} %add_rsqrt_fusion, f32[256]{0:T(256)S(1)} %broadcast_multiply_fusion, bf16[256,704]{1,0:T(8,128)(2,1)S(1)} %bitcast.70, ...), kind=kOutput, calls=%fused_computation.47 | convolution fusion | flops 2036170752 | bytes 11558913 | tf_op jit(solution)/shard_map/dot_general | solution.py:151
  69.9 12.2 %all-gather.2.cloned.1.call-done = bf16[1408,2816]{1,0:T(8,128)(2,1)} async-done(((bf16[88,2816]{1,0:T(8,128)(2,1)}), bf16[1408,2816]{1,0:T(8,128)(2,1)}) %all-gather.2.cloned.1.call-update) | async-done | bytes 7929872 | tf_op jit(solution)/shard_map/all_gather | solution.py:99
  82.0 8.3 %fusion.10 = (f32[2816]{0:T(1024)S(1)}, f32[2816]{0:T(1024)S(1)}, bf16[256,2816]{1,0:T(8,128)(2,1)}, f32[256,2816]{1,0:T(8,128)}) fusion(f32[256]{0:T(256)S(1)} %convert_element_type.365, f32[256,2816]{1,0:T(8,128)} %convolution_add_fusion, bf16[1408,2816]{1,0:T(8,128)(2,1)} %all-gather.2.cloned.1.call-done, ...), kind=kOutput, calls=%fused_computation.58 | convolution fusion | flops 2041211392 | bytes 15883265 | tf_op jit(solution)/shard_map/dot_general | solution.py:159
  90.3 48.0 %all-reduce.2 = (f32[2816]{0:T(1024)S(1)}, f32[2816]{0:T(1024)S(1)}) all-reduce(f32[2816]{0:T(1024)S(1)} %get-tuple-element.4, f32[2816]{0:T(1024)S(1)} %get-tuple-element.5), channel_id=1, replica_groups=mesh['sy'=4,'sx'=4,'tp'=2] {'sy','sx'}, use_global_device_ids=true, to_apply=%region_16.17 | all-reduce | flops 5632 | bytes 45056 | tf_op jit(solution)/shard_map/psum | solution.py:61
  139.7 1.4 collective-permute-start.5
  156.7 1.1 collective-permute-done.8
  159.8 6.3 %fusion.16 = f32[256,1408]{1,0:T(8,128)S(1)} fusion(bf16[1408,2816]{1,0:T(8,128)(2,1)} %all-gather.2.cloned.1.call-done, bf16[256,2816]{1,0:T(8,128)(2,1)} %get-tuple-element.69, f32[2816]{0:T(1024)S(1)} %copy-done.7, f32[2816]{0:T(1024)S(1)} %get-tuple-element.68, f32[2816]{0:T(1024)S(1)} %copy-done.3), kind=kOutput, calls=%fused_computation.109 | convolution fusion | flops 2034368512 | bytes 10847232 | tf_op jit(solution)/shard_map/dot_general | solution.py:164
  167.0 6.9 %fusion.102 = (f32[256]{0:T(256)S(1)}, f32[256]{0:T(256)S(1)}, f32[256,1408]{1,0:T(8,128)S(1)}, f32[256,1408]{1,0:T(8,128)S(1)}) fusion(f32[256]{0:T(256)S(1)} %add_rsqrt_fusion, f32[256]{0:T(256)S(1)} %broadcast_multiply_fusion, bf16[256,704]{1,0:T(8,128)(2,1)S(1)} %bitcast.71, bf16[256,704]{1,0:T(8,128)(2,1)S(1)} %collective-permute-done.4, ...), kind=kOutput, calls=%fused_computation.322 | convolution fusion | flops 2047344128 | bytes 18787840 | tf_op jit(solution)/shard_map/dot_general | solution.py:179
  173.9 1.4 collective-permute-start.10
  176.2 1.4 collective-permute-done.10
  177.7 5.7 %collective-permute-done.9 = bf16[256,704]{1,0:T(8,128)(2,1)S(1)} collective-permute-done((bf16[256,704]{1,0:T(8,128)(2,1)S(1)}, bf16[256,704]{1,0:T(8,128)(2,1)S(1)}, u32[]{:S(2)}, u32[]{:S(2)}) %collective-permute-start.9) | collective-permute-done | bytes 360480 | tf_op jit(solution)/shard_map/ppermute | solution.py:57
  183.4 0.9 multiply_convert_fusion.1
  184.5 10.4 %collective-permute-start.12 = (bf16[3,16,704]{2,1,0:T(8,128)(2,1)S(1)}, bf16[3,16,704]{2,1,0:T(8,128)(2,1)S(1)}, u32[]{:S(2)}, u32[]{:S(2)}) collective-permute-start(bf16[3,16,704]{2,1,0:T(8,128)(2,1)S(1)} %fusion.93), channel_id=1, source_target_pairs={{8,0},{16,8},{24,16},{9,1},{17,9},{25,17},{10,2},{18,10},{26,18},{... | collective-permute-start | bytes 202760 | tf_op jit(solution)/shard_map/ppermute | solution.py:20
  194.9 1.9 collective-permute-start.11
  197.0 1.0 fusion.28
  197.9 3.2 %collective-permute-done.11 = bf16[3,16,704]{2,1,0:T(8,128)(2,1)S(1)} collective-permute-done((bf16[3,16,704]{2,1,0:T(8,128)(2,1)S(1)}, bf16[3,16,704]{2,1,0:T(8,128)(2,1)S(1)}, u32[]{:S(2)}, u32[]{:S(2)}) %collective-permute-start.11) | collective-permute-done | bytes 67616 | tf_op jit(solution)/shard_map/ppermute | solution.py:17
  201.4 1.9 collective-permute-start.13
  203.3 2.4 %collective-permute-start.14 = (bf16[30,3,704]{2,1,0:T(4,128)(2,1)S(1)}, bf16[30,3,704]{2,1,0:T(4,128)(2,1)S(1)}, u32[]{:S(2)}, u32[]{:S(2)}) collective-permute-start(bf16[30,3,704]{2,1,0:T(4,128)(2,1)S(1)} %get-tuple-element.84), channel_id=1, source_target_pairs={{0,2},{2,4},{4,6},{1,3},{3,5},{5,7},{8,10},{10,12},{12,14},{9,11},... | collective-permute-start | bytes 380168 | tf_op jit(solution)/shard_map/ppermute | solution.py:17
  206.4 7.1 %collective-permute-done.14 = bf16[30,3,704]{2,1,0:T(4,128)(2,1)S(1)} collective-permute-done((bf16[30,3,704]{2,1,0:T(4,128)(2,1)S(1)}, bf16[30,3,704]{2,1,0:T(4,128)(2,1)S(1)}, u32[]{:S(2)}, u32[]{:S(2)}) %collective-permute-start.14) | collective-permute-done | bytes 126752 | tf_op jit(solution)/shard_map/ppermute | solution.py:17
  213.5 14.9 %add_convert_fusion.1 = bf16[24,16,704]{2,1,0:T(8,128)(2,1)} fusion(bf16[24,16,704]{2,1,0:T(8,128)(2,1)S(1)} %copy-done.1, bf16[30,16,704]{2,1,0:T(8,128)(2,1)S(1)} %constant_dynamic-update-slice_fusion.3, bf16[30,3,704]{2,1,0:T(4,128)(2,1)S(1)} %collective-permute-done.14, bf16[30,3,704]{2,1,0:T(4,128)(2,1)S(1)} %collective-permute-done.13, ...), kind=kLoop, calls=%fused_computation.130 | loop fusion | flops 77316096 | bytes 5933312 | tf_op jit(solution)/shard_map/convert_element_type | solution.py:196
  (91 shorter events, 17.5 us)
Async XLA Ops:
  7.2 24.6 %copy-start.1 = (bf16[24,16,704]{2,1,0:T(8,128)(2,1)S(1)}, bf16[24,16,704]{2,1,0:T(8,128)(2,1)}, u32[]{:S(2)}) copy-start(bf16[24,16,704]{2,1,0:T(8,128)(2,1)} %param.25) | copy-start | bytes 1622020
  7.2 74.8 %all-gather.2.cloned.1.call-start = ((), (), s32[]{:S(2)}) async-start(), calls=%async_computation | async-start | bytes 8425472 | tf_op jit(solution)/shard_map/all_gather | solution.py:99
  7.9 23.9 %copy-start.2 = (f32[7,7,704]{2,1,0:T(8,128)S(1)}, f32[7,7,704]{2,1,0:T(8,128)}, u32[]{:S(2)}) copy-start(f32[7,7,704]{2,1,0:T(8,128)} %param.14) | copy-start | bytes 413956
  8.9 23.2 %copy-start = (bf16[24,16,704]{2,1,0:T(8,128)(2,1)S(1)}, bf16[24,16,704]{2,1,0:T(8,128)(2,1)}, u32[]{:S(2)}) copy-start(bf16[24,16,704]{2,1,0:T(8,128)(2,1)} %param.13) | copy-start | bytes 1622020
  8.9 23.2 %collective-permute-start = (bf16[3,16,704]{2,1,0:T(8,128)(2,1)S(1)}, bf16[3,16,704]{2,1,0:T(8,128)(2,1)S(1)}, u32[]{:S(2)}, u32[]{:S(2)}) collective-permute-start(bf16[3,16,704]{2,1,0:T(8,128)(2,1)S(1)} %get-tuple-element.90), channel_id=1, source_target_pairs={{0,8},{8,16},{16,24},{1,9},{9,17},{17,25},{2,10},{10,18},{18,26},{... | collective-permute-start | bytes 202760 | tf_op jit(solution)/shard_map/ppermute | solution.py:17
  12.5 19.7 %collective-permute-start.1 = (bf16[3,16,704]{2,1,0:T(8,128)(2,1)S(1)}, bf16[3,16,704]{2,1,0:T(8,128)(2,1)S(1)}, u32[]{:S(2)}, u32[]{:S(2)}) collective-permute-start(bf16[3,16,704]{2,1,0:T(8,128)(2,1)S(1)} %get-tuple-element.89), channel_id=1, source_target_pairs={{8,0},{16,8},{24,16},{9,1},{17,9},{25,17},{10,2},{18,10},{26,18},{... | collective-permute-start | bytes 202760 | tf_op jit(solution)/shard_map/ppermute | solution.py:20
  32.4 6.9 %collective-permute-start.2 = (bf16[30,3,704]{2,1,0:T(4,128)(2,1)S(1)}, bf16[30,3,704]{2,1,0:T(4,128)(2,1)S(1)}, u32[]{:S(2)}, u32[]{:S(2)}) collective-permute-start(bf16[30,3,704]{2,1,0:T(4,128)(2,1)S(1)} %get-tuple-element.85), channel_id=1, source_target_pairs={{0,2},{2,4},{4,6},{1,3},{3,5},{5,7},{8,10},{10,12},{12,14},{9,11},... | collective-permute-start | bytes 380168 | tf_op jit(solution)/shard_map/ppermute | solution.py:17
  34.3 6.7 %collective-permute-start.3 = (bf16[30,3,704]{2,1,0:T(4,128)(2,1)S(1)}, bf16[30,3,704]{2,1,0:T(4,128)(2,1)S(1)}, u32[]{:S(2)}, u32[]{:S(2)}) collective-permute-start(bf16[30,3,704]{2,1,0:T(4,128)(2,1)S(1)} %get-tuple-element.86), channel_id=1, source_target_pairs={{2,0},{4,2},{6,4},{3,1},{5,3},{7,5},{10,8},{12,10},{14,12},{11,9},... | collective-permute-start | bytes 380168 | tf_op jit(solution)/shard_map/ppermute | solution.py:20
  42.3 0.7 copy-start.4
  48.8 13.4 %copy-start.6 = (f32[2816]{0:T(1024)S(1)}, f32[2816]{0:T(1024)}, u32[]{:S(2)}) copy-start(f32[2816]{0:T(1024)} %param.19) | copy-start | bytes 33796
  48.8 13.4 %copy-start.8 = (f32[1408]{0:T(1024)S(1)}, f32[1408]{0:T(1024)}, u32[]{:S(2)}) copy-start(f32[1408]{0:T(1024)} %param.17) | copy-start | bytes 16900
  48.8 13.4 %copy-start.9 = (f32[1408]{0:T(1024)S(1)}, f32[1408]{0:T(1024)}, u32[]{:S(2)}) copy-start(f32[1408]{0:T(1024)} %param.16) | copy-start | bytes 16900
  48.8 12.1 %collective-permute-start.4 = (bf16[256,704]{1,0:T(8,128)(2,1)S(1)}, bf16[256,704]{1,0:T(8,128)(2,1)S(1)}, u32[]{:S(2)}, u32[]{:S(2)}) collective-permute-start(bf16[256,704]{1,0:T(8,128)(2,1)S(1)} %bitcast.67), channel_id=1, source_target_pairs={{0,1},{1,0},{2,3},{3,2},{4,5},{5,4},{6,7},{7,6},{8,9},{9,8},{10,11... | collective-permute-start | bytes 1081352 | tf_op jit(solution)/shard_map/ppermute | solution.py:57
  50.5 19.3 %collective-permute-start.7 = (bf16[256,704]{1,0:T(8,128)(2,1)S(1)}, bf16[256,704]{1,0:T(8,128)(2,1)S(1)}, u32[]{:S(2)}, u32[]{:S(2)}) collective-permute-start(bf16[256,704]{1,0:T(8,128)(2,1)S(1)} %fusion.29), channel_id=1, source_target_pairs={{0,1},{1,0},{2,3},{3,2},{4,5},{5,4},{6,7},{7,6},{8,9},{9,8},{10,11... | collective-permute-start | bytes 1081352 | tf_op jit(solution)/shard_map/ppermute | solution.py:57
  69.9 68.5 %copy-start.3 = (f32[2816]{0:T(1024)S(1)}, f32[2816]{0:T(1024)}, u32[]{:S(2)}) copy-start(f32[2816]{0:T(1024)} %param.20) | copy-start | bytes 33796
  69.9 89.9 %copy-start.7 = (f32[2816]{0:T(1024)S(1)}, f32[2816]{0:T(1024)}, u32[]{:S(2)}) copy-start(f32[2816]{0:T(1024)} %param.21) | copy-start | bytes 33796
  139.7 15.2 %collective-permute-start.5 = (f32[8,128]{1,0:T(8,128)S(1)}, f32[8,128]{1,0:T(8,128)S(1)}, u32[]{:S(2)}, u32[]{:S(2)}) collective-permute-start(f32[8,128]{1,0:T(8,128)S(1)} %broadcast_in_dim.16), channel_id=1, source_target_pairs={{0,1},{1,0},{2,3},{3,2},{4,5},{5,4},{6,7},{7,6},{8,9},{9,8},{10,11... | collective-permute-start | bytes 12296 | tf_op jit(solution)/shard_map/ppermute | solution.py:57
  154.2 3.7 %collective-permute-start.8 = (f32[8,128]{1,0:T(8,128)S(1)}, f32[8,128]{1,0:T(8,128)S(1)}, u32[]{:S(2)}, u32[]{:S(2)}) collective-permute-start(f32[8,128]{1,0:T(8,128)S(1)} %broadcast_in_dim.17), channel_id=1, source_target_pairs={{0,1},{1,0},{2,3},{3,2},{4,5},{5,4},{6,7},{7,6},{8,9},{9,8},{10,11... | collective-permute-start | bytes 12296 | tf_op jit(solution)/shard_map/ppermute | solution.py:57
  159.7 7.2 %copy-start.10 = (f32[256,2816]{1,0:T(8,128)S(1)}, f32[256,2816]{1,0:T(8,128)}, u32[]{:S(2)}) copy-start(f32[256,2816]{1,0:T(8,128)} %convolution_add_fusion) | copy-start | bytes 8650756
  159.8 7.2 %copy-start.11 = (f32[256,2816]{1,0:T(8,128)S(1)}, f32[256,2816]{1,0:T(8,128)}, u32[]{:S(2)}) copy-start(f32[256,2816]{1,0:T(8,128)} %get-tuple-element.114) | copy-start | bytes 8650756
  159.8 7.2 %copy-start.12 = (bf16[256,2816]{1,0:T(8,128)(2,1)S(1)}, bf16[256,2816]{1,0:T(8,128)(2,1)}, u32[]{:S(2)}) copy-start(bf16[256,2816]{1,0:T(8,128)(2,1)} %get-tuple-element.69) | copy-start | bytes 4325380
  166.2 11.4 %collective-permute-start.6 = (bf16[256,704]{1,0:T(8,128)(2,1)S(1)}, bf16[256,704]{1,0:T(8,128)(2,1)S(1)}, u32[]{:S(2)}, u32[]{:S(2)}) collective-permute-start(bf16[256,704]{1,0:T(8,128)(2,1)S(1)} %dynamic-slice_convert_fusion.1), channel_id=1, source_target_pairs={{0,1},{1,0},{2,3},{3,2},{4,5},{5,4},{6,7},{7,6},{8,9},{9,8},{10,11... | collective-permute-start | bytes 1081352 | tf_op jit(solution)/shard_map/ppermute | solution.py:57
  167.0 16.4 %copy-start.5 = (f32[704]{0:T(1024)S(1)}, f32[704]{0:T(1024)}, u32[]{:S(2)}) copy-start(f32[704]{0:T(1024)} %param.23) | copy-start | bytes 8452
  173.9 3.7 %collective-permute-start.10 = (f32[2,256]{1,0:T(2,128)S(1)}, f32[2,256]{1,0:T(2,128)S(1)}, u32[]{:S(2)}, u32[]{:S(2)}) collective-permute-start(f32[2,256]{1,0:T(2,128)S(1)} %pad_maximum_fusion.8), channel_id=1, source_target_pairs={{0,1},{1,0},{2,3},{3,2},{4,5},{5,4},{6,7},{7,6},{8,9},{9,8},{10,11... | collective-permute-start | bytes 6152 | tf_op jit(solution)/shard_map/ppermute | solution.py:57
  175.5 7.8 %collective-permute-start.9 = (bf16[256,704]{1,0:T(8,128)(2,1)S(1)}, bf16[256,704]{1,0:T(8,128)(2,1)S(1)}, u32[]{:S(2)}, u32[]{:S(2)}) collective-permute-start(bf16[256,704]{1,0:T(8,128)(2,1)S(1)} %dynamic-slice_convert_fusion), channel_id=1, source_target_pairs={{0,1},{1,0},{2,3},{3,2},{4,5},{5,4},{6,7},{7,6},{8,9},{9,8},{10,11... | collective-permute-start | bytes 1081352 | tf_op jit(solution)/shard_map/ppermute | solution.py:57
  184.5 16.8 %collective-permute-start.12 = (bf16[3,16,704]{2,1,0:T(8,128)(2,1)S(1)}, bf16[3,16,704]{2,1,0:T(8,128)(2,1)S(1)}, u32[]{:S(2)}, u32[]{:S(2)}) collective-permute-start(bf16[3,16,704]{2,1,0:T(8,128)(2,1)S(1)} %fusion.93), channel_id=1, source_target_pairs={{8,0},{16,8},{24,16},{9,1},{17,9},{25,17},{10,2},{18,10},{26,18},{... | collective-permute-start | bytes 202760 | tf_op jit(solution)/shard_map/ppermute | solution.py:20
  194.9 6.2 %collective-permute-start.11 = (bf16[3,16,704]{2,1,0:T(8,128)(2,1)S(1)}, bf16[3,16,704]{2,1,0:T(8,128)(2,1)S(1)}, u32[]{:S(2)}, u32[]{:S(2)}) collective-permute-start(bf16[3,16,704]{2,1,0:T(8,128)(2,1)S(1)} %fusion.94), channel_id=1, source_target_pairs={{0,8},{8,16},{16,24},{1,9},{9,17},{17,25},{2,10},{10,18},{18,26},{... | collective-permute-start | bytes 202760 | tf_op jit(solution)/shard_map/ppermute | solution.py:17
  201.4 5.0 %collective-permute-start.13 = (bf16[30,3,704]{2,1,0:T(4,128)(2,1)S(1)}, bf16[30,3,704]{2,1,0:T(4,128)(2,1)S(1)}, u32[]{:S(2)}, u32[]{:S(2)}) collective-permute-start(bf16[30,3,704]{2,1,0:T(4,128)(2,1)S(1)} %get-tuple-element.83), channel_id=1, source_target_pairs={{2,0},{4,2},{6,4},{3,1},{5,3},{7,5},{10,8},{12,10},{14,12},{11,9},... | collective-permute-start | bytes 380168 | tf_op jit(solution)/shard_map/ppermute | solution.py:20
  203.3 10.2 %collective-permute-start.14 = (bf16[30,3,704]{2,1,0:T(4,128)(2,1)S(1)}, bf16[30,3,704]{2,1,0:T(4,128)(2,1)S(1)}, u32[]{:S(2)}, u32[]{:S(2)}) collective-permute-start(bf16[30,3,704]{2,1,0:T(4,128)(2,1)S(1)} %get-tuple-element.84), channel_id=1, source_target_pairs={{0,2},{2,4},{4,6},{1,3},{3,5},{5,7},{8,10},{10,12},{12,14},{9,11},... | collective-permute-start | bytes 380168 | tf_op jit(solution)/shard_map/ppermute | solution.py:17
Sparse Core Ops, SparseCore 0:
  10.2 71.7 all-gather.1
where the time goes:
time: 236 us; the launch traced here: 235 us
  blocking collectives  48 us (20%)
  waiting for transfers between devices  43.9 us (19%)
  between operations  37.6 us (16%)
  starting transfers between devices  35.4 us (15%)
  other arithmetic  33.5 us (14%)
  matrix products  29.1 us (12%)
  local copies, waits for them, and re-layouts  7.66 us (3%)
    psum x1, blocking collectives, over_pixels(): return lax.psum(vector, ('sy', 'sx'))  48 us
    ppermute x4, starting transfers between devices, extended(): lax.ppermute(lax.slice_in_dim(block, 0, width, axis=dim), axis, backward)  18.3 us
    ppermute x7, waiting for transfers between devices, swapped(): return lax.ppermute(array, 'tp', [(i, count - 1 - i) for i in range(count)])  17.4 us
    convert_element_type x1, other arithmetic, shards(): feature_grad = (cotangent.astype(jnp.float32) + depthwise(extend(grad_ima...  14.9 us
    all_gather x1, waiting for transfers between devices, shards(): down_t = lax.all_gather(down_weight.T, ('sy', 'sx'), axis=0, tiled=True)  12.2 us
    ppermute x4, waiting for transfers between devices, extended(): lax.ppermute(lax.slice_in_dim(block, block.shape[dim] - width, None, axis...  11.4 us
    ppermute x4, starting transfers between devices, extended(): lax.ppermute(lax.slice_in_dim(block, block.shape[dim] - width, None, axis...  9.87 us
    dot_general x1, matrix products, shards(): back_hidden = jnp.dot(cot_wide, down_t, preferred_element_type=jnp.float32)  8.27 us
  transfers between devices with their start and end apart: 16, of which 10 were waited for; matrix products, arithmetic and copies ran while one was open for 15% of the time, Pallas kernels for 0%

commit v1 on v0

--- a/solution.py
+++ b/solution.py
@@ -58,7 +58,7 @@
 
 
 def over_pixels(vector):
-    return lax.psum(vector, ("sy", "sx"))
+    return jnp.sum(lax.all_gather(vector, ("sy", "sx")), axis=0)
 
 
 def conv_tiles(windows, kernel):

time: 236 us -> 218 us (0.924)
  blocking collectives: 48 us -> 36.2 us
  starting transfers between devices: 35.4 us -> 30.1 us
    psum x1 -> x0, blocking collectives: 48 us -> none  [over_pixels(): return lax.psum(vector, ('sy', 'sx'))]
    all_gather x0 -> x2, blocking collectives: none -> 36.2 us  [over_pixels(): return jnp.sum(lax.all_gather(vector, ('sy', 'sx')), axis=0)]
    ppermute x4, starting transfers between devices: 18.3 us -> 13.1 us  [extended(): lax.ppermute(lax.slice_in_dim(block, 0, width, axis=dim), axis, backward)]
    ppermute x4, waiting for transfers between devices: 11.4 us -> 8.13 us  [extended(): lax.ppermute(lax.slice_in_dim(block, block.shape[dim] - width, None, axis...]
  transfers between devices with their start and end apart: 16 -> 16, of which waited for: 10 -> 10; matrix products, arithmetic and copies ran while one was open for 15% -> 17% of each run, Pallas kernels for 0% -> 0%
where the time goes in v1:
time: 218 us; the launch traced here: 217 us
  waiting for transfers between devices  42.3 us (19%)
  between operations  37.7 us (17%)
  blocking collectives  36.2 us (17%)
  other arithmetic  33.7 us (15%)
  starting transfers between devices  30.1 us (14%)
  matrix products  29.1 us (13%)
  local copies, waits for them, and re-layouts  7.69 us (4%)
    all_gather x2, blocking collectives, over_pixels(): return jnp.sum(lax.all_gather(vector, ('sy', 'sx')), axis=0)  36.2 us
    ppermute x7, waiting for transfers between devices, swapped(): return lax.ppermute(array, 'tp', [(i, count - 1 - i) for i in range(count)])  19 us
    convert_element_type x1, other arithmetic, shards(): feature_grad = (cotangent.astype(jnp.float32) + depthwise(extend(grad_ima...  14.9 us
    ppermute x4, starting transfers between devices, extended(): lax.ppermute(lax.slice_in_dim(block, 0, width, axis=dim), axis, backward)  13.1 us
    all_gather x1, waiting for transfers between devices, shards(): down_t = lax.all_gather(down_weight.T, ('sy', 'sx'), axis=0, tiled=True)  12.1 us
    ppermute x4, starting transfers between devices, extended(): lax.ppermute(lax.slice_in_dim(block, block.shape[dim] - width, None, axis...  9.87 us
    dot_general x1, matrix products, shards(): back_hidden = jnp.dot(cot_wide, down_t, preferred_element_type=jnp.float32)  8.26 us
    ppermute x4, waiting for transfers between devices, extended(): lax.ppermute(lax.slice_in_dim(block, block.shape[dim] - width, None, axis...  8.13 us
  transfers between devices with their start and end apart: 16, of which 10 were waited for; matrix products, arithmetic and copies ran while one was open for 17% of the time, Pallas kernels for 0%

profile of v1, /device:TPU:12, one launch (start us, length us, event | category | flops | bytes accessed | tf_op | source)
XLA Modules:
  0.0 216.7 jit_solution(18354878049924046646)
XLA Ops:
  7.9 1.0 fusion.105
  8.9 3.6 %collective-permute-start = (bf16[3,16,704]{2,1,0:T(8,128)(2,1)S(1)}, bf16[3,16,704]{2,1,0:T(8,128)(2,1)S(1)}, u32[]{:S(2)}, u32[]{:S(2)}) collective-permute-start(bf16[3,16,704]{2,1,0:T(8,128)(2,1)S(1)} %get-tuple-element.88), channel_id=1, source_target_pairs={{0,8},{8,16},{16,24},{1,9},{9,17},{17,25},{2,10},{10,18},{18,26},{... | collective-permute-start | bytes 202760 | tf_op jit(solution)/shard_map/ppermute | solution.py:17
  12.5 2.4 %collective-permute-start.1 = (bf16[3,16,704]{2,1,0:T(8,128)(2,1)S(1)}, bf16[3,16,704]{2,1,0:T(8,128)(2,1)S(1)}, u32[]{:S(2)}, u32[]{:S(2)}) collective-permute-start(bf16[3,16,704]{2,1,0:T(8,128)(2,1)S(1)} %get-tuple-element.87), channel_id=1, source_target_pairs={{8,0},{16,8},{24,16},{9,1},{17,9},{25,17},{10,2},{18,10},{26,18},{... | collective-permute-start | bytes 202760 | tf_op jit(solution)/shard_map/ppermute | solution.py:20
  15.9 1.3 reduce_sum.184
  28.8 2.7 %add_convert_fusion.4 = f32[4]{0:T(128)S(1)} fusion(s32[1]{0:T(128)} %bitcast.3, s32[1]{0:T(128)} %bitcast.2, s32[1]{0:T(128)} %bitcast.1, s32[1]{0:T(128)} %bitcast), kind=kLoop, calls=%fused_computation.313 | loop fusion | flops 16 | bytes 32 | tf_op jit(solution)/shard_map/convert_element_type | solution.py:107
  32.4 1.9 collective-permute-start.2
  34.3 3.6 %collective-permute-start.3 = (bf16[30,3,704]{2,1,0:T(4,128)(2,1)S(1)}, bf16[30,3,704]{2,1,0:T(4,128)(2,1)S(1)}, u32[]{:S(2)}, u32[]{:S(2)}) collective-permute-start(bf16[30,3,704]{2,1,0:T(4,128)(2,1)S(1)} %get-tuple-element.84), channel_id=1, source_target_pairs={{2,0},{4,2},{6,4},{3,1},{5,3},{7,5},{10,8},{12,10},{14,12},{11,9},... | collective-permute-start | bytes 380168 | tf_op jit(solution)/shard_map/ppermute | solution.py:20
  38.1 1.1 collective-permute-done.2
  39.2 1.8 collective-permute-done.3
  43.0 5.8 %add_convert_fusion.2 = bf16[4,8,8,704]{3,2,1,0:T(8,128)(2,1)S(1)} fusion(bf16[4,14,14,704]{3,2,1,0:T(8,128)(2,1)S(1)} %pad_maximum_fusion, f32[704]{0:T(1024)S(1)} %copy-done.4, f32[704]{0:T(1024)S(1)} %get-tuple-element.53, f32[704]{0:T(1024)S(1)} %get-tuple-element.54, f32[704]{0:T(1024)S(1)} %get-tuple-element.7, f32[704]{0:T(1024)S(1)} %get-tuple-element.8, ...), kind=kLoop, calls=%fused_computation.138 | loop fusion | flops 26673152 | bytes 18163200 | tf_op jit(solution)/shard_map/convert_element_type | solution.py:144
  48.8 1.6 collective-permute-start.4
  51.8 9.1 %collective-permute-done.4 = bf16[256,704]{1,0:T(8,128)(2,1)S(1)} collective-permute-done((bf16[256,704]{1,0:T(8,128)(2,1)S(1)}, bf16[256,704]{1,0:T(8,128)(2,1)S(1)}, u32[]{:S(2)}, u32[]{:S(2)}) %collective-permute-start.4) | collective-permute-done | bytes 360480 | tf_op jit(solution)/shard_map/ppermute | solution.py:57
  62.2 7.7 %convolution_add_fusion = f32[256,2816]{1,0:T(8,128)} fusion(bf16[1408,2816]{1,0:T(8,128)(2,1)} %param.18, f32[2816]{0:T(1024)S(1)} %copy-done.6, f32[1408]{0:T(1024)S(1)} %copy-done.8, f32[1408]{0:T(1024)S(1)} %copy-done.9, f32[256]{0:T(256)S(1)} %add_rsqrt_fusion, f32[256]{0:T(256)S(1)} %broadcast_multiply_fusion, bf16[256,704]{1,0:T(8,128)(2,1)S(1)} %bitcast.70, ...), kind=kOutput, calls=%fused_computation.47 | convolution fusion | flops 2036170752 | bytes 11558913 | tf_op jit(solution)/shard_map/dot_general | solution.py:151
  69.9 12.1 %all-gather.6.cloned.1.call-done = bf16[1408,2816]{1,0:T(8,128)(2,1)} async-done(((bf16[88,2816]{1,0:T(8,128)(2,1)}), bf16[1408,2816]{1,0:T(8,128)(2,1)}) %all-gather.6.cloned.1.call-update) | async-done | bytes 7929872 | tf_op jit(solution)/shard_map/all_gather | solution.py:99
  82.0 8.3 %fusion.10 = (f32[2816]{0:T(1024)S(1)}, f32[2816]{0:T(1024)S(1)}, bf16[256,2816]{1,0:T(8,128)(2,1)}, f32[256,2816]{1,0:T(8,128)}) fusion(f32[256]{0:T(256)S(1)} %convert_element_type.365, f32[256,2816]{1,0:T(8,128)} %convolution_add_fusion, bf16[1408,2816]{1,0:T(8,128)(2,1)} %all-gather.6.cloned.1.call-done, ...), kind=kOutput, calls=%fused_computation.58 | convolution fusion | flops 2041211392 | bytes 15883265 | tf_op jit(solution)/shard_map/dot_general | solution.py:159
  90.3 16.8 %all-gather.2 = f32[16,1,2816]{2,1,0:T(1,128)S(1)} all-gather(f32[1,1,2816]{2,1,0:T(1,128)S(1)} %reshape.145), channel_id=2, replica_groups=mesh['sy'=4,'sx'=4,'tp'=2] {'sy','sx'}, dimensions={0}, use_global_device_ids=true | all-gather | bytes 191488 | tf_op jit(solution)/shard_map/all_gather | solution.py:61
  107.0 19.5 %all-gather.3 = f32[16,1,2816]{2,1,0:T(1,128)S(1)} all-gather(f32[1,1,2816]{2,1,0:T(1,128)S(1)} %reshape.147), channel_id=3, replica_groups=mesh['sy'=4,'sx'=4,'tp'=2] {'sy','sx'}, dimensions={0}, use_global_device_ids=true | all-gather | bytes 191488 | tf_op jit(solution)/shard_map/all_gather | solution.py:61
  128.1 1.5 collective-permute-start.5
  145.2 1.2 collective-permute-done.8
  148.3 6.3 %fusion.16 = f32[256,1408]{1,0:T(8,128)S(1)} fusion(bf16[1408,2816]{1,0:T(8,128)(2,1)} %all-gather.6.cloned.1.call-done, bf16[256,2816]{1,0:T(8,128)(2,1)} %get-tuple-element.67, f32[2816]{0:T(1024)S(1)} %copy-done.7, f32[2816]{0:T(1024)S(1)} %get-tuple-element.66, f32[2816]{0:T(1024)S(1)} %copy-done.3), kind=kOutput, calls=%fused_computation.109 | convolution fusion | flops 2034368512 | bytes 10847232 | tf_op jit(solution)/shard_map/dot_general | solution.py:164
  155.4 6.9 %fusion.102 = (f32[256]{0:T(256)S(1)}, f32[256]{0:T(256)S(1)}, f32[256,1408]{1,0:T(8,128)S(1)}, f32[256,1408]{1,0:T(8,128)S(1)}) fusion(f32[256]{0:T(256)S(1)} %add_rsqrt_fusion, f32[256]{0:T(256)S(1)} %broadcast_multiply_fusion, bf16[256,704]{1,0:T(8,128)(2,1)S(1)} %bitcast.71, bf16[256,704]{1,0:T(8,128)(2,1)S(1)} %collective-permute-done.4, ...), kind=kOutput, calls=%fused_computation.322 | convolution fusion | flops 2047344128 | bytes 18787840 | tf_op jit(solution)/shard_map/dot_general | solution.py:179
  162.3 1.5 collective-permute-start.10
  164.6 1.3 collective-permute-done.10
  166.0 7.4 %collective-permute-done.9 = bf16[256,704]{1,0:T(8,128)(2,1)S(1)} collective-permute-done((bf16[256,704]{1,0:T(8,128)(2,1)S(1)}, bf16[256,704]{1,0:T(8,128)(2,1)S(1)}, u32[]{:S(2)}, u32[]{:S(2)}) %collective-permute-start.9) | collective-permute-done | bytes 360480 | tf_op jit(solution)/shard_map/ppermute | solution.py:57
  174.5 5.2 %collective-permute-start.12 = (bf16[3,16,704]{2,1,0:T(8,128)(2,1)S(1)}, bf16[3,16,704]{2,1,0:T(8,128)(2,1)S(1)}, u32[]{:S(2)}, u32[]{:S(2)}) collective-permute-start(bf16[3,16,704]{2,1,0:T(8,128)(2,1)S(1)} %fusion.93), channel_id=1, source_target_pairs={{8,0},{16,8},{24,16},{9,1},{17,9},{25,17},{10,2},{18,10},{26,18},{... | collective-permute-start | bytes 202760 | tf_op jit(solution)/shard_map/ppermute | solution.py:20
  179.7 1.9 collective-permute-start.11
  181.8 1.0 fusion.28
  182.7 3.2 %collective-permute-done.11 = bf16[3,16,704]{2,1,0:T(8,128)(2,1)S(1)} collective-permute-done((bf16[3,16,704]{2,1,0:T(8,128)(2,1)S(1)}, bf16[3,16,704]{2,1,0:T(8,128)(2,1)S(1)}, u32[]{:S(2)}, u32[]{:S(2)}) %collective-permute-start.11) | collective-permute-done | bytes 67616 | tf_op jit(solution)/shard_map/ppermute | solution.py:17
  186.2 1.9 collective-permute-start.13
  188.1 2.4 %collective-permute-start.14 = (bf16[30,3,704]{2,1,0:T(4,128)(2,1)S(1)}, bf16[30,3,704]{2,1,0:T(4,128)(2,1)S(1)}, u32[]{:S(2)}, u32[]{:S(2)}) collective-permute-start(bf16[30,3,704]{2,1,0:T(4,128)(2,1)S(1)} %get-tuple-element.82), channel_id=1, source_target_pairs={{0,2},{2,4},{4,6},{1,3},{3,5},{5,7},{8,10},{10,12},{12,14},{9,11},... | collective-permute-start | bytes 380168 | tf_op jit(solution)/shard_map/ppermute | solution.py:17
  191.2 3.8 %collective-permute-done.14 = bf16[30,3,704]{2,1,0:T(4,128)(2,1)S(1)} collective-permute-done((bf16[30,3,704]{2,1,0:T(4,128)(2,1)S(1)}, bf16[30,3,704]{2,1,0:T(4,128)(2,1)S(1)}, u32[]{:S(2)}, u32[]{:S(2)}) %collective-permute-start.14) | collective-permute-done | bytes 126752 | tf_op jit(solution)/shard_map/ppermute | solution.py:17
  195.0 14.9 %add_convert_fusion.1 = bf16[24,16,704]{2,1,0:T(8,128)(2,1)} fusion(bf16[24,16,704]{2,1,0:T(8,128)(2,1)S(1)} %copy-done.1, bf16[30,16,704]{2,1,0:T(8,128)(2,1)S(1)} %constant_dynamic-update-slice_fusion.3, bf16[30,3,704]{2,1,0:T(4,128)(2,1)S(1)} %collective-permute-done.14, bf16[30,3,704]{2,1,0:T(4,128)(2,1)S(1)} %collective-permute-done.13, ...), kind=kLoop, calls=%fused_computation.130 | loop fusion | flops 77316096 | bytes 5933312 | tf_op jit(solution)/shard_map/convert_element_type | solution.py:196
  (96 shorter events, 18.6 us)
Async XLA Ops:
  7.2 24.6 %copy-start.1 = (bf16[24,16,704]{2,1,0:T(8,128)(2,1)S(1)}, bf16[24,16,704]{2,1,0:T(8,128)(2,1)}, u32[]{:S(2)}) copy-start(bf16[24,16,704]{2,1,0:T(8,128)(2,1)} %param.25) | copy-start | bytes 1622020
  7.2 74.8 %all-gather.6.cloned.1.call-start = ((), (), s32[]{:S(2)}) async-start(), calls=%async_computation | async-start | bytes 8425472 | tf_op jit(solution)/shard_map/all_gather | solution.py:99
  7.9 23.9 %copy-start.2 = (f32[7,7,704]{2,1,0:T(8,128)S(1)}, f32[7,7,704]{2,1,0:T(8,128)}, u32[]{:S(2)}) copy-start(f32[7,7,704]{2,1,0:T(8,128)} %param.14) | copy-start | bytes 413956
  8.9 23.2 %copy-start = (bf16[24,16,704]{2,1,0:T(8,128)(2,1)S(1)}, bf16[24,16,704]{2,1,0:T(8,128)(2,1)}, u32[]{:S(2)}) copy-start(bf16[24,16,704]{2,1,0:T(8,128)(2,1)} %param.13) | copy-start | bytes 1622020
  8.9 23.2 %collective-permute-start = (bf16[3,16,704]{2,1,0:T(8,128)(2,1)S(1)}, bf16[3,16,704]{2,1,0:T(8,128)(2,1)S(1)}, u32[]{:S(2)}, u32[]{:S(2)}) collective-permute-start(bf16[3,16,704]{2,1,0:T(8,128)(2,1)S(1)} %get-tuple-element.88), channel_id=1, source_target_pairs={{0,8},{8,16},{16,24},{1,9},{9,17},{17,25},{2,10},{10,18},{18,26},{... | collective-permute-start | bytes 202760 | tf_op jit(solution)/shard_map/ppermute | solution.py:17
  12.5 19.7 %collective-permute-start.1 = (bf16[3,16,704]{2,1,0:T(8,128)(2,1)S(1)}, bf16[3,16,704]{2,1,0:T(8,128)(2,1)S(1)}, u32[]{:S(2)}, u32[]{:S(2)}) collective-permute-start(bf16[3,16,704]{2,1,0:T(8,128)(2,1)S(1)} %get-tuple-element.87), channel_id=1, source_target_pairs={{8,0},{16,8},{24,16},{9,1},{17,9},{25,17},{10,2},{18,10},{26,18},{... | collective-permute-start | bytes 202760 | tf_op jit(solution)/shard_map/ppermute | solution.py:20
  32.4 6.9 %collective-permute-start.2 = (bf16[30,3,704]{2,1,0:T(4,128)(2,1)S(1)}, bf16[30,3,704]{2,1,0:T(4,128)(2,1)S(1)}, u32[]{:S(2)}, u32[]{:S(2)}) collective-permute-start(bf16[30,3,704]{2,1,0:T(4,128)(2,1)S(1)} %get-tuple-element.83), channel_id=1, source_target_pairs={{0,2},{2,4},{4,6},{1,3},{3,5},{5,7},{8,10},{10,12},{12,14},{9,11},... | collective-permute-start | bytes 380168 | tf_op jit(solution)/shard_map/ppermute | solution.py:17
  34.3 6.7 %collective-permute-start.3 = (bf16[30,3,704]{2,1,0:T(4,128)(2,1)S(1)}, bf16[30,3,704]{2,1,0:T(4,128)(2,1)S(1)}, u32[]{:S(2)}, u32[]{:S(2)}) collective-permute-start(bf16[30,3,704]{2,1,0:T(4,128)(2,1)S(1)} %get-tuple-element.84), channel_id=1, source_target_pairs={{2,0},{4,2},{6,4},{3,1},{5,3},{7,5},{10,8},{12,10},{14,12},{11,9},... | collective-permute-start | bytes 380168 | tf_op jit(solution)/shard_map/ppermute | solution.py:20
  42.3 0.7 copy-start.4
  48.8 13.4 %copy-start.6 = (f32[2816]{0:T(1024)S(1)}, f32[2816]{0:T(1024)}, u32[]{:S(2)}) copy-start(f32[2816]{0:T(1024)} %param.19) | copy-start | bytes 33796
  48.8 13.4 %copy-start.8 = (f32[1408]{0:T(1024)S(1)}, f32[1408]{0:T(1024)}, u32[]{:S(2)}) copy-start(f32[1408]{0:T(1024)} %param.17) | copy-start | bytes 16900
  48.8 13.4 %copy-start.9 = (f32[1408]{0:T(1024)S(1)}, f32[1408]{0:T(1024)}, u32[]{:S(2)}) copy-start(f32[1408]{0:T(1024)} %param.16) | copy-start | bytes 16900
  48.8 12.1 %collective-permute-start.4 = (bf16[256,704]{1,0:T(8,128)(2,1)S(1)}, bf16[256,704]{1,0:T(8,128)(2,1)S(1)}, u32[]{:S(2)}, u32[]{:S(2)}) collective-permute-start(bf16[256,704]{1,0:T(8,128)(2,1)S(1)} %bitcast.67), channel_id=1, source_target_pairs={{0,1},{1,0},{2,3},{3,2},{4,5},{5,4},{6,7},{7,6},{8,9},{9,8},{10,11... | collective-permute-start | bytes 1081352 | tf_op jit(solution)/shard_map/ppermute | solution.py:57
  50.5 19.3 %collective-permute-start.7 = (bf16[256,704]{1,0:T(8,128)(2,1)S(1)}, bf16[256,704]{1,0:T(8,128)(2,1)S(1)}, u32[]{:S(2)}, u32[]{:S(2)}) collective-permute-start(bf16[256,704]{1,0:T(8,128)(2,1)S(1)} %fusion.29), channel_id=1, source_target_pairs={{0,1},{1,0},{2,3},{3,2},{4,5},{5,4},{6,7},{7,6},{8,9},{9,8},{10,11... | collective-permute-start | bytes 1081352 | tf_op jit(solution)/shard_map/ppermute | solution.py:57
  69.9 56.9 %copy-start.3 = (f32[2816]{0:T(1024)S(1)}, f32[2816]{0:T(1024)}, u32[]{:S(2)}) copy-start(f32[2816]{0:T(1024)} %param.20) | copy-start | bytes 33796
  69.9 78.4 %copy-start.7 = (f32[2816]{0:T(1024)S(1)}, f32[2816]{0:T(1024)}, u32[]{:S(2)}) copy-start(f32[2816]{0:T(1024)} %param.21) | copy-start | bytes 33796
  128.1 15.2 %collective-permute-start.5 = (f32[8,128]{1,0:T(8,128)S(1)}, f32[8,128]{1,0:T(8,128)S(1)}, u32[]{:S(2)}, u32[]{:S(2)}) collective-permute-start(f32[8,128]{1,0:T(8,128)S(1)} %broadcast_in_dim.16), channel_id=1, source_target_pairs={{0,1},{1,0},{2,3},{3,2},{4,5},{5,4},{6,7},{7,6},{8,9},{9,8},{10,11... | collective-permute-start | bytes 12296 | tf_op jit(solution)/shard_map/ppermute | solution.py:57
  142.7 3.7 %collective-permute-start.8 = (f32[8,128]{1,0:T(8,128)S(1)}, f32[8,128]{1,0:T(8,128)S(1)}, u32[]{:S(2)}, u32[]{:S(2)}) collective-permute-start(f32[8,128]{1,0:T(8,128)S(1)} %broadcast_in_dim.17), channel_id=1, source_target_pairs={{0,1},{1,0},{2,3},{3,2},{4,5},{5,4},{6,7},{7,6},{8,9},{9,8},{10,11... | collective-permute-start | bytes 12296 | tf_op jit(solution)/shard_map/ppermute | solution.py:57
  148.2 7.2 %copy-start.10 = (f32[256,2816]{1,0:T(8,128)S(1)}, f32[256,2816]{1,0:T(8,128)}, u32[]{:S(2)}) copy-start(f32[256,2816]{1,0:T(8,128)} %convolution_add_fusion) | copy-start | bytes 8650756
  148.2 7.2 %copy-start.11 = (f32[256,2816]{1,0:T(8,128)S(1)}, f32[256,2816]{1,0:T(8,128)}, u32[]{:S(2)}) copy-start(f32[256,2816]{1,0:T(8,128)} %get-tuple-element.112) | copy-start | bytes 8650756
  148.2 7.2 %copy-start.12 = (bf16[256,2816]{1,0:T(8,128)(2,1)S(1)}, bf16[256,2816]{1,0:T(8,128)(2,1)}, u32[]{:S(2)}) copy-start(bf16[256,2816]{1,0:T(8,128)(2,1)} %get-tuple-element.67) | copy-start | bytes 4325380
  154.7 11.3 %collective-permute-start.6 = (bf16[256,704]{1,0:T(8,128)(2,1)S(1)}, bf16[256,704]{1,0:T(8,128)(2,1)S(1)}, u32[]{:S(2)}, u32[]{:S(2)}) collective-permute-start(bf16[256,704]{1,0:T(8,128)(2,1)S(1)} %dynamic-slice_convert_fusion.1), channel_id=1, source_target_pairs={{0,1},{1,0},{2,3},{3,2},{4,5},{5,4},{6,7},{7,6},{8,9},{9,8},{10,11... | collective-permute-start | bytes 1081352 | tf_op jit(solution)/shard_map/ppermute | solution.py:57
  155.4 18.0 %copy-start.5 = (f32[704]{0:T(1024)S(1)}, f32[704]{0:T(1024)}, u32[]{:S(2)}) copy-start(f32[704]{0:T(1024)} %param.23) | copy-start | bytes 8452
  162.3 3.7 %collective-permute-start.10 = (f32[2,256]{1,0:T(2,128)S(1)}, f32[2,256]{1,0:T(2,128)S(1)}, u32[]{:S(2)}, u32[]{:S(2)}) collective-permute-start(f32[2,256]{1,0:T(2,128)S(1)} %pad_maximum_fusion.8), channel_id=1, source_target_pairs={{0,1},{1,0},{2,3},{3,2},{4,5},{5,4},{6,7},{7,6},{8,9},{9,8},{10,11... | collective-permute-start | bytes 6152 | tf_op jit(solution)/shard_map/ppermute | solution.py:57
  164.0 9.5 %collective-permute-start.9 = (bf16[256,704]{1,0:T(8,128)(2,1)S(1)}, bf16[256,704]{1,0:T(8,128)(2,1)S(1)}, u32[]{:S(2)}, u32[]{:S(2)}) collective-permute-start(bf16[256,704]{1,0:T(8,128)(2,1)S(1)} %dynamic-slice_convert_fusion), channel_id=1, source_target_pairs={{0,1},{1,0},{2,3},{3,2},{4,5},{5,4},{6,7},{7,6},{8,9},{9,8},{10,11... | collective-permute-start | bytes 1081352 | tf_op jit(solution)/shard_map/ppermute | solution.py:57
  174.5 11.5 %collective-permute-start.12 = (bf16[3,16,704]{2,1,0:T(8,128)(2,1)S(1)}, bf16[3,16,704]{2,1,0:T(8,128)(2,1)S(1)}, u32[]{:S(2)}, u32[]{:S(2)}) collective-permute-start(bf16[3,16,704]{2,1,0:T(8,128)(2,1)S(1)} %fusion.93), channel_id=1, source_target_pairs={{8,0},{16,8},{24,16},{9,1},{17,9},{25,17},{10,2},{18,10},{26,18},{... | collective-permute-start | bytes 202760 | tf_op jit(solution)/shard_map/ppermute | solution.py:20
  179.7 6.2 %collective-permute-start.11 = (bf16[3,16,704]{2,1,0:T(8,128)(2,1)S(1)}, bf16[3,16,704]{2,1,0:T(8,128)(2,1)S(1)}, u32[]{:S(2)}, u32[]{:S(2)}) collective-permute-start(bf16[3,16,704]{2,1,0:T(8,128)(2,1)S(1)} %fusion.94), channel_id=1, source_target_pairs={{0,8},{8,16},{16,24},{1,9},{9,17},{17,25},{2,10},{10,18},{18,26},{... | collective-permute-start | bytes 202760 | tf_op jit(solution)/shard_map/ppermute | solution.py:17
  186.2 5.0 %collective-permute-start.13 = (bf16[30,3,704]{2,1,0:T(4,128)(2,1)S(1)}, bf16[30,3,704]{2,1,0:T(4,128)(2,1)S(1)}, u32[]{:S(2)}, u32[]{:S(2)}) collective-permute-start(bf16[30,3,704]{2,1,0:T(4,128)(2,1)S(1)} %get-tuple-element.81), channel_id=1, source_target_pairs={{2,0},{4,2},{6,4},{3,1},{5,3},{7,5},{10,8},{12,10},{14,12},{11,9},... | collective-permute-start | bytes 380168 | tf_op jit(solution)/shard_map/ppermute | solution.py:20
  188.1 6.9 %collective-permute-start.14 = (bf16[30,3,704]{2,1,0:T(4,128)(2,1)S(1)}, bf16[30,3,704]{2,1,0:T(4,128)(2,1)S(1)}, u32[]{:S(2)}, u32[]{:S(2)}) collective-permute-start(bf16[30,3,704]{2,1,0:T(4,128)(2,1)S(1)} %get-tuple-element.82), channel_id=1, source_target_pairs={{0,2},{2,4},{4,6},{1,3},{3,5},{5,7},{8,10},{10,12},{12,14},{9,11},... | collective-permute-start | bytes 380168 | tf_op jit(solution)/shard_map/ppermute | solution.py:17
Sparse Core Ops, SparseCore 0:
  10.2 71.7 all-gather.5
